TPU v7x, 32 devices: a whole 2x2x4 slice. The times are simulated.
32 devices in a mesh: dom: 8 (over z, y), span: 4 (over x, core).
Axes of the slice: x: 2, y: 2, z: 4, core: 2. Of those that a mesh axis runs over, the one named last changes fastest.
Arguments:
- entities: bfloat16 [8192, 256], P('dom'), may hold values from -2.5 to 2.5
- operators: bfloat16 [64, 256, 256], P('span'), may hold values from -0.375 to 0.375
- left_rows: int32 [3, 8, 4, 512], P(None, 'dom', 'span'), may hold values from 0 to 1023
- right_rows: int32 [3, 8, 4, 512], P(None, 'dom', 'span'), may hold values from 0 to 1023
- negatives: int32 [3, 8, 4, 1024], P(None, 'dom', 'span'), may hold values from 0 to 1023
- counts: int32 [3, 8, 4, 64], P(None, 'dom', 'span'), may hold values from 1 to 8, as said below
Outputs:
- entity_grad: float32 [8192, 256], P(('dom', 'span'))
- relation_grad: float32 [64, 256, 256], P('span', 'dom')
Inputs may be any that keep to these rules, and one draw needn't show every extreme that they name: `counts`: in every bucket step and partition one relation has all 8 slots live in every group's list.
All inputs are finite; a program needn't handle non-finite values.
Results may differ from a plain program's by a relative error of at most 0.0021.
Values may be sent and summed in bfloat16 or wider, within the bound.
A program may use at most 64 MiB of HBM per device.

v0:
```python
import functools

import jax
import jax.numpy as jnp
from jax import lax
from jax.experimental import pallas as pl
from jax.experimental.pallas import tpu as pltpu
from jax.sharding import PartitionSpec as P

MESH = pl.DeviceIdType.MESH
F32 = jnp.float32
BF16 = jnp.bfloat16
LANES = 128
MULT_AT = 16


def dot(a, b, dims):
    return lax.dot_general(a, b, (dims, ((), ())), preferred_element_type=F32)


def rounded(value):
    return value.astype(BF16).astype(F32)


def kernel(
    dims,
    ent,
    ops,
    left_rows,
    right_rows,
    negatives,
    counts,
    ent_out,
    rel_out,
    slabs,
    meta_send,
    meta,
    cols,
    onehot,
    lefts,
    queries,
    query_grads,
    acc,
    own_grad,
    grad_send,
    grad_recv,
    home_send,
    home_recv,
    rel_acc,
    y_send,
    y_recv,
    z_send,
    z_recv,
    meta_ss,
    meta_rs,
    slab_ss,
    slab_rs,
    grad_ss,
    grad_rs,
    home_ss,
    home_rs,
    y_ss,
    y_rs,
    z_ss,
    z_rs,
):
    buckets, doms, groups, rel_own, cap, chunks = dims
    part_rows, width = ent.shape
    slot_count = left_rows.shape[1]
    neg_count = negatives.shape[1]
    relations = rel_own * groups
    slots = rel_own * cap
    levels = doms // 2
    own_rows = part_rows // groups
    out_rows = width // doms
    chunk_rels = rel_own // chunks
    chunk_rows = chunk_rels * out_rows
    mult_rows = part_rows // LANES
    neg_scale = float(neg_count) ** (-0.5)
    dom = lax.axis_index("dom")
    span = lax.axis_index("span")
    y = lax.rem(dom, 2)
    z = lax.div(dom, 2)

    def span_peer(offset):
        return (dom, lax.rem(span + offset, groups))

    def dom_peer(offset):
        return (lax.rem(dom + offset + doms, doms), span)

    def send(src, dst, send_sem, recv_sem, peer):
        copy = pltpu.make_async_remote_copy(
            src_ref=src,
            dst_ref=dst,
            send_sem=send_sem,
            recv_sem=recv_sem,
            device_id=peer,
            device_id_type=MESH,
        )
        copy.start()
        return copy

    barrier = pltpu.get_barrier_semaphore()
    for offset in range(1, groups):
        pl.semaphore_signal(barrier, inc=1, device_id=span_peer(offset), device_id_type=MESH)
    for offset in range(1, doms):
        pl.semaphore_signal(barrier, inc=1, device_id=dom_peer(offset), device_id_type=MESH)

    expand = (
        lax.broadcasted_iota(jnp.int32, (relations, slot_count), 1) // cap
        == lax.broadcasted_iota(jnp.int32, (relations, slot_count), 0)
    )
    wide_counts = dot(
        counts[...].astype(F32).astype(BF16),
        jnp.where(expand, 1.0, 0.0).astype(BF16),
        ((1,), (0,)),
    )
    place = (lax.broadcasted_iota(jnp.int32, (buckets, slot_count), 1) % cap).astype(F32)
    live = jnp.where(wide_counts > place, 1.0, 0.0)
    left_wide = left_rows[...].astype(F32)
    right_wide = right_rows[...].astype(F32)
    meta_send[...] = jnp.zeros(meta_send.shape, F32)
    for holder in range(groups):
        cut = slice(holder * slots, (holder + 1) * slots)
        meta_send[holder, 0:buckets, 0:slots] = left_wide[:, cut]
        meta_send[holder, buckets : 2 * buckets, 0:slots] = right_wide[:, cut]
        meta_send[holder, 2 * buckets : 3 * buckets, 0:slots] = live[:, cut]
    for bucket in range(buckets):
        row = negatives[bucket : bucket + 1, :]
        high = lax.broadcasted_iota(jnp.int32, (mult_rows, neg_count), 0) == row // LANES
        low = lax.broadcasted_iota(jnp.int32, (LANES, neg_count), 0) == row % LANES
        mult = dot(
            jnp.where(high, 1.0, 0.0).astype(BF16),
            jnp.where(low, 1.0, 0.0).astype(BF16),
            ((1,), (1,)),
        )
        at = MULT_AT + bucket * mult_rows
        for holder in range(groups):
            meta_send[holder, at : at + mult_rows, :] = mult

    pl.semaphore_wait(barrier, groups - 1 + doms - 1)
    meta_copies = []
    for offset in range(1, groups):
        peer = span_peer(offset)
        meta_copies.append(
            send(meta_send.at[peer[1]], meta.at[offset], meta_ss.at[offset], meta_rs.at[offset], peer)
        )
    slab_copies = [
        send(ent, slabs.at[b - 1], slab_ss.at[b - 1], slab_rs.at[b - 1], dom_peer(-b))
        for b in range(1, buckets)
    ]
    meta[0] = meta_send[span]
    for copy in meta_copies:
        copy.wait()

    lane_row = lax.broadcasted_iota(jnp.int32, (slots, part_rows), 1).astype(F32)
    for group in range(groups):
        cols[group] = jnp.transpose(meta[group, 0:MULT_AT, :])
    for bucket in range(buckets):
        for group in range(groups):
            hit = lane_row == cols[group, 0:slots, bucket : bucket + 1]
            onehot[bucket, group * slots : (group + 1) * slots, :] = jnp.where(hit, 1.0, 0.0).astype(BF16)
        picked = dot(onehot[bucket], ent[...], ((1,), (0,)))
        for group in range(groups):
            at = (bucket * groups + group) * cap
            lefts[:, at : at + cap, :] = picked[group * slots : (group + 1) * slots].reshape(rel_own, cap, width)

    def apply_operator(rel, _):
        queries[rel] = rounded(dot(lefts[rel].astype(BF16), ops[rel], ((1,), (0,))))
        return _

    lax.fori_loop(0, rel_own, apply_operator, 0)

    acc[...] = jnp.zeros(acc.shape, F32)

    def score(bucket, right):
        def one_group(group, _):
            at = pl.multiple_of((bucket * groups + group) * cap, cap)
            query = queries[:, pl.ds(at, cap), :].reshape(slots, width).astype(BF16)
            right_col = cols[group, 0:slots, buckets + bucket : buckets + bucket + 1]
            live_col = cols[group, 0:slots, 2 * buckets + bucket : 2 * buckets + bucket + 1]
            first = MULT_AT + bucket * mult_rows
            mult = jnp.concatenate(
                [meta[group, first + part : first + part + 1, :] for part in range(mult_rows)], axis=1
            )
            scores = dot(query, right[...], ((1,), (1,)))
            hit = lane_row == right_col
            positive = jnp.sum(jnp.where(hit, scores, 0.0), axis=1, keepdims=True)
            pos_grad = -live_col * jax.nn.sigmoid(-positive)
            neg_grad = rounded((jnp.tanh(scores * 0.5) + 1.0) * (live_col * (0.5 * neg_scale)))
            weight = neg_grad * mult + jnp.where(hit, pos_grad, 0.0)
            high = weight.astype(BF16)
            low = (weight - high.astype(F32)).astype(BF16)
            both = jnp.concatenate([high, low], axis=0)
            parts = dot(both, right[...], ((1,), (0,)))
            query_grad = rounded(parts[0:slots] + parts[slots:])
            query_grads[:, pl.ds(at, cap), :] = query_grad.reshape(rel_own, cap, width)
            twice = jnp.concatenate([query, query], axis=0)
            acc[bucket] += dot(twice, both, ((0,), (0,)))
            return _

        lax.fori_loop(0, groups, one_group, 0)

    def send_grads(bucket):
        total = jnp.transpose(acc[bucket])
        own_grad[bucket] = total
        for holder in range(groups):
            grad_send[bucket, holder] = total[holder * own_rows : (holder + 1) * own_rows].astype(BF16)
        copies = []
        for offset in range(1, groups):
            peer = span_peer(offset)
            copies.append(
                send(
                    grad_send.at[bucket, peer[1]],
                    grad_recv.at[bucket, offset],
                    grad_ss.at[bucket, offset],
                    grad_rs.at[bucket, offset],
                    peer,
                )
            )
        return copies

    def gathered(bucket, copies):
        for copy in copies:
            copy.wait()
        total = own_grad[bucket, pl.ds(pl.multiple_of(span * own_rows, own_rows), own_rows), :]
        for offset in range(1, groups):
            total = total + grad_recv[bucket, offset].astype(F32)
        return total

    score(0, ent)
    grad_copies = [None]
    for bucket in range(1, buckets):
        slab_copies[bucket - 1].wait()
        score(bucket, slabs.at[bucket - 1])

    y_copies = []
    for chunk in range(chunks):

        def one_relation(rel, _):
            outer = dot(lefts[rel].astype(BF16), query_grads[rel].astype(BF16), ((0,), (0,)))
            at = pl.multiple_of(rel * out_rows, out_rows)
            for level in range(levels):
                for side in range(2):
                    first = (level * 2 + side) * out_rows
                    rel_acc[side, level, pl.ds(at, out_rows), :] = outer[first : first + out_rows]
            return _

        lax.fori_loop(chunk * chunk_rels, (chunk + 1) * chunk_rels, one_relation, 0)
        rows = slice(chunk * chunk_rows, (chunk + 1) * chunk_rows)
        y_send[chunk] = rel_acc[1 - y, :, rows, :].astype(BF16)
        y_copies.append(
            send(y_send.at[chunk], y_recv.at[chunk], y_ss.at[chunk], y_rs.at[chunk], (dom + 1 - 2 * y, span))
        )

    for bucket in range(1, buckets):
        grad_copies.append(send_grads(bucket))

    def apply_transposed(rel, _):
        queries[rel] = rounded(dot(query_grads[rel].astype(BF16), ops[rel], ((1,), (1,))))
        return _

    lax.fori_loop(0, rel_own, apply_transposed, 0)

    z_copies = []

    def send_level(chunk):
        y_copies[chunk].wait()
        rows = slice(chunk * chunk_rows, (chunk + 1) * chunk_rows)
        total = rel_acc[y, :, rows, :] + y_recv[chunk].astype(F32)
        rel_acc[y, :, rows, :] = total
        z_send[chunk] = total.astype(BF16)
        for offset in range(1, levels):
            level = lax.rem(z + offset, levels)
            z_copies.append(
                send(
                    z_send.at[chunk, level],
                    z_recv.at[chunk, offset],
                    z_ss.at[chunk, offset],
                    z_rs.at[chunk, offset],
                    (level * 2 + y, span),
                )
            )

    send_level(0)
    for bucket in range(buckets):
        grad_rows = jnp.concatenate(
            [
                queries[:, (bucket * groups + group) * cap : (bucket * groups + group + 1) * cap, :].reshape(slots, width)
                for group in range(groups)
            ],
            axis=0,
        ).astype(BF16)
        acc[0] += dot(grad_rows, onehot[bucket], ((0,), (0,)))
    grad_copies[0] = send_grads(0)
    send_level(1)

    home_copies = []
    for bucket in range(1, buckets):
        home_send[bucket] = gathered(bucket, grad_copies[bucket])
        home_copies.append(
            send(home_send.at[bucket], home_recv.at[bucket], home_ss.at[bucket], home_rs.at[bucket], dom_peer(bucket))
        )
    for chunk in range(2, chunks):
        send_level(chunk)

    total = gathered(0, grad_copies[0])
    for bucket in range(1, buckets):
        home_copies[bucket - 1].wait()
        total = total + home_recv[bucket]
    ent_out[...] = total

    for chunk in range(chunks):
        for copy in z_copies[chunk * (levels - 1) : (chunk + 1) * (levels - 1)]:
            copy.wait()
        rows = slice(chunk * chunk_rows, (chunk + 1) * chunk_rows)
        total = rel_acc[y, z, rows, :]
        for offset in range(1, levels):
            total = total + z_recv[chunk, offset].astype(F32)
        rel_out[rows, :] = total


def shards(entities, operators, left_rows, right_rows, negatives, counts):
    buckets = left_rows.shape[0]
    slot_count = left_rows.shape[-1]
    neg_count = negatives.shape[-1]
    groups = lax.axis_size("span")
    doms = lax.axis_size("dom")
    rel_own = operators.shape[0]
    relations = rel_own * groups
    cap = slot_count // relations
    slots = rel_own * cap
    part_rows, width = entities.shape
    own_rows = part_rows // groups
    out_rows = width // doms
    levels = doms // 2
    chunks = 4 if (rel_own // 4) * out_rows % 16 == 0 else 2
    chunk_rows = rel_own // chunks * out_rows
    mult_rows = part_rows // LANES
    meta_rows = MULT_AT + -(-buckets * mult_rows // 8) * 8
    edges = buckets * groups * cap
    dims = (buckets, doms, groups, rel_own, cap, chunks)
    dma = pltpu.SemaphoreType.DMA
    vmem = pl.BlockSpec(memory_space=pltpu.VMEM)
    ent_grad, rel_grad = pl.pallas_call(
        functools.partial(kernel, dims),
        out_shape=(
            jax.ShapeDtypeStruct((own_rows, width), F32),
            jax.ShapeDtypeStruct((rel_own * out_rows, width), F32),
        ),
        in_specs=[vmem] * 6,
        out_specs=(vmem, vmem),
        scratch_shapes=[
            pltpu.VMEM((buckets - 1, part_rows, width), BF16),
            pltpu.VMEM((groups, meta_rows, LANES), F32),
            pltpu.VMEM((groups, meta_rows, LANES), F32),
            pltpu.VMEM((groups, LANES, MULT_AT), F32),
            pltpu.VMEM((buckets, groups * slots, part_rows), BF16),
            pltpu.VMEM((rel_own, edges, width), F32),
            pltpu.VMEM((rel_own, edges, width), F32),
            pltpu.VMEM((rel_own, edges, width), F32),
            pltpu.VMEM((buckets, width, part_rows), F32),
            pltpu.VMEM((buckets, part_rows, width), F32),
            pltpu.VMEM((buckets, groups, own_rows, width), BF16),
            pltpu.VMEM((buckets, groups, own_rows, width), BF16),
            pltpu.VMEM((buckets, own_rows, width), F32),
            pltpu.VMEM((buckets, own_rows, width), F32),
            pltpu.VMEM((2, levels, rel_own * out_rows, width), F32),
            pltpu.VMEM((chunks, levels, chunk_rows, width), BF16),
            pltpu.VMEM((chunks, levels, chunk_rows, width), BF16),
            pltpu.VMEM((chunks, levels, chunk_rows, width), BF16),
            pltpu.VMEM((chunks, levels, chunk_rows, width), BF16),
            dma((groups,)),
            dma((groups,)),
            dma((buckets - 1,)),
            dma((buckets - 1,)),
            dma((buckets, groups)),
            dma((buckets, groups)),
            dma((buckets,)),
            dma((buckets,)),
            dma((chunks,)),
            dma((chunks,)),
            dma((chunks, levels)),
            dma((chunks, levels)),
        ],
        compiler_params=pltpu.CompilerParams(
            collective_id=0, has_side_effects=True, vmem_limit_bytes=58 * 1024 * 1024
        ),
        name="train_step",
    )(
        entities,
        operators,
        left_rows.reshape(buckets, slot_count),
        right_rows.reshape(buckets, slot_count),
        negatives.reshape(buckets, neg_count),
        counts.reshape(buckets, relations),
    )
    return (ent_grad, rel_grad.reshape(rel_own, out_rows, width))


def solution(mesh):
    in_specs = (
        P("dom", None),
        P("span", None, None),
        P(None, "dom", "span", None),
        P(None, "dom", "span", None),
        P(None, "dom", "span", None),
        P(None, "dom", "span", None),
    )
    out_specs = (P(("dom", "span"), None), P("span", "dom", None))
    return jax.shard_map(shards, mesh=mesh, in_specs=in_specs, out_specs=out_specs, check_vma=False)
```

profile of v0, /device:TPU:4, one launch (start us, length us, event | category | flops | bytes accessed | tf_op | source)
XLA Modules:
  0.0 85.3 jit_solution(3922244071804933254)
XLA Ops:
  0.6 1.3 %copy.17 = s32[3,1,1,64]{3,0,1,2:T(4,128)} copy(s32[3,1,1,64]{3,2,1,0:T(1,128)} %param.11) | data formatting | bytes 1536
  1.9 1.3 %copy.16 = s32[3,1,1,1024]{3,0,1,2:T(4,128)} copy(s32[3,1,1,1024]{3,2,1,0:T(1,128)} %param.10) | data formatting | bytes 24576
  3.2 1.3 %copy_bitcast_fusion.1 = (s32[3,512]{1,0:T(4,128)}, s32[3,512]{1,0:T(4,128)}) fusion(s32[3,1,1,512]{3,2,1,0:T(1,128)} %param.9, s32[3,1,1,512]{3,2,1,0:T(1,128)} %param.8), kind=kLoop, calls=%fused_computation.1 | loop fusion | bytes 24576
  4.5 77.2 %train_step.1 = (f32[256,256]{1,0:T(8,128)}, f32[512,256]{1,0:T(8,128)}) custom-call(bf16[1024,256]{1,0:T(8,128)(2,1)} %ent.1, bf16[16,256,256]{2,1,0:T(8,128)(2,1)} %ops.1, s32[3,512]{1,0:T(4,128)} %get-tuple-element.7.left_rows, s32[3,512]{1,0:T(4,128)} %get-tuple-element.6.right_rows, s32[3,1024]{1,0:T(4,128)} %bitcast.12, s32[3,64]{1,0:T(4,128)} %bitcast.13), custom_call_target="tpu_custom_call" | custom-call | tf_op jit(solution)/shard_map/train_step/pallas_call | solution.py:345
  81.7 1.7 %copy.20 = f32[256,256]{1,0:T(8,128)} copy(f32[256,256]{1,0:T(8,128)} %get-tuple-element.10) | data formatting | bytes 524288
  83.4 1.9 %copy.21 = f32[16,32,256]{2,1,0:T(8,128)} copy(f32[16,32,256]{2,1,0:T(8,128)} %bitcast.11) | data formatting | bytes 1048576
where the time goes:
time: 85.6 us; the launch traced here: 85.3 us
  Pallas kernels  77.2 us (90%)
  local copies, waits for them, and re-layouts  7.43 us (9%)
    pallas_call x1, Pallas kernels, shards(): pl.pallas_call(functools.partial(kernel, dims), out_shape=(jax.ShapeDtype...  77.2 us
    unnamed x5, local copies, waits for them, and re-layouts  7.43 us

commit v1 on v0

--- a/solution.py
+++ b/solution.py
@@ -36,6 +36,7 @@
     meta_send,
     meta,
     cols,
+    times,
     onehot,
     lefts,
     queries,
@@ -66,8 +67,8 @@
 ):
     buckets, doms, groups, rel_own, cap, chunks = dims
     part_rows, width = ent.shape
-    slot_count = left_rows.shape[1]
-    neg_count = negatives.shape[1]
+    slot_count = left_rows.shape[-1]
+    neg_count = negatives.shape[-1]
     relations = rel_own * groups
     slots = rel_own * cap
     levels = doms // 2
@@ -75,6 +76,8 @@
     out_rows = width // doms
     chunk_rels = rel_own // chunks
     chunk_rows = chunk_rels * out_rows
+    share = groups * cap
+    block = chunk_rels * share
     mult_rows = part_rows // LANES
     neg_scale = float(neg_count) ** (-0.5)
     dom = lax.axis_index("dom")
@@ -106,19 +109,22 @@
     for offset in range(1, doms):
         pl.semaphore_signal(barrier, inc=1, device_id=dom_peer(offset), device_id_type=MESH)
 
+    def rows_of(ref):
+        return jnp.concatenate([ref[bucket, 0] for bucket in range(buckets)], axis=0)
+
     expand = (
         lax.broadcasted_iota(jnp.int32, (relations, slot_count), 1) // cap
         == lax.broadcasted_iota(jnp.int32, (relations, slot_count), 0)
     )
     wide_counts = dot(
-        counts[...].astype(F32).astype(BF16),
+        rows_of(counts).astype(F32).astype(BF16),
         jnp.where(expand, 1.0, 0.0).astype(BF16),
         ((1,), (0,)),
     )
     place = (lax.broadcasted_iota(jnp.int32, (buckets, slot_count), 1) % cap).astype(F32)
     live = jnp.where(wide_counts > place, 1.0, 0.0)
-    left_wide = left_rows[...].astype(F32)
-    right_wide = right_rows[...].astype(F32)
+    left_wide = rows_of(left_rows).astype(F32)
+    right_wide = rows_of(right_rows).astype(F32)
     meta_send[...] = jnp.zeros(meta_send.shape, F32)
     for holder in range(groups):
         cut = slice(holder * slots, (holder + 1) * slots)
@@ -126,7 +132,7 @@
         meta_send[holder, buckets : 2 * buckets, 0:slots] = right_wide[:, cut]
         meta_send[holder, 2 * buckets : 3 * buckets, 0:slots] = live[:, cut]
     for bucket in range(buckets):
-        row = negatives[bucket : bucket + 1, :]
+        row = negatives[bucket, 0]
         high = lax.broadcasted_iota(jnp.int32, (mult_rows, neg_count), 0) == row // LANES
         low = lax.broadcasted_iota(jnp.int32, (LANES, neg_count), 0) == row % LANES
         mult = dot(
@@ -153,53 +159,100 @@
     for copy in meta_copies:
         copy.wait()
 
-    lane_row = lax.broadcasted_iota(jnp.int32, (slots, part_rows), 1).astype(F32)
+    lane_row = lax.broadcasted_iota(jnp.int32, (block, part_rows), 1).astype(F32)
     for group in range(groups):
-        cols[group] = jnp.transpose(meta[group, 0:MULT_AT, :])
-    for bucket in range(buckets):
-        for group in range(groups):
-            hit = lane_row == cols[group, 0:slots, bucket : bucket + 1]
-            onehot[bucket, group * slots : (group + 1) * slots, :] = jnp.where(hit, 1.0, 0.0).astype(BF16)
-        picked = dot(onehot[bucket], ent[...], ((1,), (0,)))
-        for group in range(groups):
-            at = (bucket * groups + group) * cap
-            lefts[:, at : at + cap, :] = picked[group * slots : (group + 1) * slots].reshape(rel_own, cap, width)
-
-    def apply_operator(rel, _):
-        queries[rel] = rounded(dot(lefts[rel].astype(BF16), ops[rel], ((1,), (0,))))
-        return _
-
-    lax.fori_loop(0, rel_own, apply_operator, 0)
-
-    acc[...] = jnp.zeros(acc.shape, F32)
-
-    def score(bucket, right):
-        def one_group(group, _):
-            at = pl.multiple_of((bucket * groups + group) * cap, cap)
-            query = queries[:, pl.ds(at, cap), :].reshape(slots, width).astype(BF16)
-            right_col = cols[group, 0:slots, buckets + bucket : buckets + bucket + 1]
-            live_col = cols[group, 0:slots, 2 * buckets + bucket : 2 * buckets + bucket + 1]
+        turned = jnp.transpose(meta[group, 0:MULT_AT, :])
+        cols[:, group * cap : (group + 1) * cap, :] = turned[0:slots].reshape(rel_own, cap, MULT_AT)
+        for bucket in range(buckets):
             first = MULT_AT + bucket * mult_rows
             mult = jnp.concatenate(
                 [meta[group, first + part : first + part + 1, :] for part in range(mult_rows)], axis=1
             )
-            scores = dot(query, right[...], ((1,), (1,)))
-            hit = lane_row == right_col
-            positive = jnp.sum(jnp.where(hit, scores, 0.0), axis=1, keepdims=True)
-            pos_grad = -live_col * jax.nn.sigmoid(-positive)
-            neg_grad = rounded((jnp.tanh(scores * 0.5) + 1.0) * (live_col * (0.5 * neg_scale)))
-            weight = neg_grad * mult + jnp.where(hit, pos_grad, 0.0)
-            high = weight.astype(BF16)
-            low = (weight - high.astype(F32)).astype(BF16)
-            both = jnp.concatenate([high, low], axis=0)
-            parts = dot(both, right[...], ((1,), (0,)))
-            query_grad = rounded(parts[0:slots] + parts[slots:])
-            query_grads[:, pl.ds(at, cap), :] = query_grad.reshape(rel_own, cap, width)
-            twice = jnp.concatenate([query, query], axis=0)
-            acc[bucket] += dot(twice, both, ((0,), (0,)))
-            return _
-
-        lax.fori_loop(0, groups, one_group, 0)
+            times[bucket, group * cap : (group + 1) * cap, :] = jnp.broadcast_to(mult, (cap, part_rows))
+
+    def column(chunk, which):
+        held = cols[chunk * chunk_rels : (chunk + 1) * chunk_rels].reshape(block, MULT_AT)
+        return held[:, which : which + 1]
+
+    for bucket in range(buckets):
+        for chunk in range(chunks):
+            hit = lane_row == column(chunk, bucket)
+            onehot[bucket, chunk * block : (chunk + 1) * block, :] = jnp.where(hit, 1.0, 0.0).astype(BF16)
+        picked = dot(onehot[bucket], ent[...], ((1,), (0,)))
+        lefts[:, bucket * share : (bucket + 1) * share, :] = picked.reshape(rel_own, share, width)
+    for rel in range(rel_own):
+        queries[rel] = rounded(dot(lefts[rel].astype(BF16), ops[rel], ((1,), (0,))))
+
+    def score(chunk, bucket):
+        right = ent if bucket == 0 else slabs.at[bucket - 1]
+        rels = slice(chunk * chunk_rels, (chunk + 1) * chunk_rels)
+        at = slice(bucket * share, (bucket + 1) * share)
+        query = queries[rels, at, :].reshape(block, width).astype(BF16)
+        live_col = column(chunk, 2 * buckets + bucket)
+        scores = dot(query, right[...], ((1,), (1,)))
+        hit = lane_row == column(chunk, buckets + bucket)
+        positive = jnp.sum(jnp.where(hit, scores, 0.0), axis=1, keepdims=True)
+        pos_grad = -live_col * jax.nn.sigmoid(-positive)
+        neg_grad = rounded((jnp.tanh(scores * 0.5) + 1.0) * (live_col * (0.5 * neg_scale)))
+        counted = neg_grad.reshape(chunk_rels, share, part_rows) * times[bucket][None]
+        weight = counted.reshape(block, part_rows) + jnp.where(hit, pos_grad, 0.0)
+        high = weight.astype(BF16)
+        low = (weight - high.astype(F32)).astype(BF16)
+        both = jnp.concatenate([high, low], axis=0)
+        parts = dot(both, right[...], ((1,), (0,)))
+        query_grad = rounded(parts[0:block] + parts[block:])
+        query_grads[rels, at, :] = query_grad.reshape(chunk_rels, share, width)
+        twice = jnp.concatenate([query, query], axis=0)
+        slab_grad = dot(twice, both, ((0,), (0,)))
+        if chunk == 0:
+            acc[bucket] = slab_grad
+        else:
+            acc[bucket] += slab_grad
+
+    y_copies = []
+
+    def send_pair(chunk):
+        for rel in range(chunk * chunk_rels, (chunk + 1) * chunk_rels):
+            outer = dot(lefts[rel].astype(BF16), query_grads[rel].astype(BF16), ((0,), (0,)))
+            for level in range(levels):
+                for side in range(2):
+                    first = (level * 2 + side) * out_rows
+                    rel_acc[side, level, rel * out_rows : (rel + 1) * out_rows, :] = outer[first : first + out_rows]
+        rows = slice(chunk * chunk_rows, (chunk + 1) * chunk_rows)
+        y_send[chunk] = rel_acc[1 - y, :, rows, :].astype(BF16)
+        y_copies.append(
+            send(y_send.at[chunk], y_recv.at[chunk], y_ss.at[chunk], y_rs.at[chunk], (dom + 1 - 2 * y, span))
+        )
+
+    z_copies = []
+
+    def send_level(chunk):
+        y_copies[chunk].wait()
+        rows = slice(chunk * chunk_rows, (chunk + 1) * chunk_rows)
+        total = rel_acc[y, :, rows, :] + y_recv[chunk].astype(F32)
+        rel_acc[y, :, rows, :] = total
+        z_send[chunk] = total.astype(BF16)
+        for offset in range(1, levels):
+            level = lax.rem(z + offset, levels)
+            z_copies.append(
+                send(
+                    z_send.at[chunk, level],
+                    z_recv.at[chunk, offset],
+                    z_ss.at[chunk, offset],
+                    z_rs.at[chunk, offset],
+                    (level * 2 + y, span),
+                )
+            )
+
+    def left_part(chunk):
+        rels = range(chunk * chunk_rels, (chunk + 1) * chunk_rels)
+        turned = [rounded(dot(query_grads[rel].astype(BF16), ops[rel], ((1,), (1,)))) for rel in rels]
+        rows, marks = [], []
+        for bucket in range(buckets):
+            rows += [value[bucket * share : (bucket + 1) * share] for value in turned]
+            marks.append(onehot[bucket, chunk * block : (chunk + 1) * block, :])
+        rows = jnp.concatenate(rows, axis=0).astype(BF16)
+        acc[0] += dot(rows, jnp.concatenate(marks, axis=0), ((0,), (0,)))
 
     def send_grads(bucket):
         total = jnp.transpose(acc[bucket])
@@ -228,72 +281,24 @@
             total = total + grad_recv[bucket, offset].astype(F32)
         return total
 
-    score(0, ent)
-    grad_copies = [None]
-    for bucket in range(1, buckets):
-        slab_copies[bucket - 1].wait()
-        score(bucket, slabs.at[bucket - 1])
-
-    y_copies = []
+    score(0, 0)
+    score(1, 0)
+    for copy in slab_copies:
+        copy.wait()
     for chunk in range(chunks):
-
-        def one_relation(rel, _):
-            outer = dot(lefts[rel].astype(BF16), query_grads[rel].astype(BF16), ((0,), (0,)))
-            at = pl.multiple_of(rel * out_rows, out_rows)
-            for level in range(levels):
-                for side in range(2):
-                    first = (level * 2 + side) * out_rows
-                    rel_acc[side, level, pl.ds(at, out_rows), :] = outer[first : first + out_rows]
-            return _
-
-        lax.fori_loop(chunk * chunk_rels, (chunk + 1) * chunk_rels, one_relation, 0)
-        rows = slice(chunk * chunk_rows, (chunk + 1) * chunk_rows)
-        y_send[chunk] = rel_acc[1 - y, :, rows, :].astype(BF16)
-        y_copies.append(
-            send(y_send.at[chunk], y_recv.at[chunk], y_ss.at[chunk], y_rs.at[chunk], (dom + 1 - 2 * y, span))
-        )
-
-    for bucket in range(1, buckets):
-        grad_copies.append(send_grads(bucket))
-
-    def apply_transposed(rel, _):
-        queries[rel] = rounded(dot(query_grads[rel].astype(BF16), ops[rel], ((1,), (1,))))
-        return _
-
-    lax.fori_loop(0, rel_own, apply_transposed, 0)
-
-    z_copies = []
-
-    def send_level(chunk):
-        y_copies[chunk].wait()
-        rows = slice(chunk * chunk_rows, (chunk + 1) * chunk_rows)
-        total = rel_acc[y, :, rows, :] + y_recv[chunk].astype(F32)
-        rel_acc[y, :, rows, :] = total
-        z_send[chunk] = total.astype(BF16)
-        for offset in range(1, levels):
-            level = lax.rem(z + offset, levels)
-            z_copies.append(
-                send(
-                    z_send.at[chunk, level],
-                    z_recv.at[chunk, offset],
-                    z_ss.at[chunk, offset],
-                    z_rs.at[chunk, offset],
-                    (level * 2 + y, span),
-                )
-            )
-
-    send_level(0)
-    for bucket in range(buckets):
-        grad_rows = jnp.concatenate(
-            [
-                queries[:, (bucket * groups + group) * cap : (bucket * groups + group + 1) * cap, :].reshape(slots, width)
-                for group in range(groups)
-            ],
-            axis=0,
-        ).astype(BF16)
-        acc[0] += dot(grad_rows, onehot[bucket], ((0,), (0,)))
+        if chunk > 1:
+            score(chunk, 0)
+        for bucket in range(1, buckets):
+            score(chunk, bucket)
+        send_pair(chunk)
+        if chunk > 0:
+            send_level(chunk - 1)
+        if chunk < chunks - 1:
+            left_part(chunk)
+    grad_copies = [None] + [send_grads(bucket) for bucket in range(1, buckets)]
+    left_part(chunks - 1)
     grad_copies[0] = send_grads(0)
-    send_level(1)
+    send_level(chunks - 1)
 
     home_copies = []
     for bucket in range(1, buckets):
@@ -301,9 +306,6 @@
         home_copies.append(
             send(home_send.at[bucket], home_recv.at[bucket], home_ss.at[bucket], home_rs.at[bucket], dom_peer(bucket))
         )
-    for chunk in range(2, chunks):
-        send_level(chunk)
-
     total = gathered(0, grad_copies[0])
     for bucket in range(1, buckets):
         home_copies[bucket - 1].wait()
@@ -320,6 +322,17 @@
         rel_out[rows, :] = total
 
 
+def hand_over(ent_grad, rel_grad, ent_out, rel_out, sems):
+    copies = [
+        pltpu.make_async_copy(ent_grad, ent_out, sems.at[0]),
+        pltpu.make_async_copy(rel_grad, rel_out, sems.at[1]),
+    ]
+    for copy in copies:
+        copy.start()
+    for copy in copies:
+        copy.wait()
+
+
 def shards(entities, operators, left_rows, right_rows, negatives, counts):
     buckets = left_rows.shape[0]
     slot_count = left_rows.shape[-1]
@@ -327,8 +340,7 @@
     groups = lax.axis_size("span")
     doms = lax.axis_size("dom")
     rel_own = operators.shape[0]
-    relations = rel_own * groups
-    cap = slot_count // relations
+    cap = slot_count // (rel_own * groups)
     slots = rel_own * cap
     part_rows, width = entities.shape
     own_rows = part_rows // groups
@@ -354,7 +366,8 @@
             pltpu.VMEM((buckets - 1, part_rows, width), BF16),
             pltpu.VMEM((groups, meta_rows, LANES), F32),
             pltpu.VMEM((groups, meta_rows, LANES), F32),
-            pltpu.VMEM((groups, LANES, MULT_AT), F32),
+            pltpu.VMEM((rel_own, groups * cap, MULT_AT), F32),
+            pltpu.VMEM((buckets, groups * cap, part_rows), F32),
             pltpu.VMEM((buckets, groups * slots, part_rows), BF16),
             pltpu.VMEM((rel_own, edges, width), F32),
             pltpu.VMEM((rel_own, edges, width), F32),
@@ -387,14 +400,20 @@
             collective_id=0, has_side_effects=True, vmem_limit_bytes=58 * 1024 * 1024
         ),
         name="train_step",
-    )(
-        entities,
-        operators,
-        left_rows.reshape(buckets, slot_count),
-        right_rows.reshape(buckets, slot_count),
-        negatives.reshape(buckets, neg_count),
-        counts.reshape(buckets, relations),
-    )
+    )(entities, operators, left_rows, right_rows, negatives, counts)
+    anywhere = pl.BlockSpec(memory_space=pl.ANY)
+    ent_grad, rel_grad = pl.pallas_call(
+        hand_over,
+        out_shape=(
+            jax.ShapeDtypeStruct(ent_grad.shape, F32),
+            jax.ShapeDtypeStruct(rel_grad.shape, F32),
+        ),
+        in_specs=[anywhere] * 2,
+        out_specs=(anywhere, anywhere),
+        scratch_shapes=[dma((2,))],
+        compiler_params=pltpu.CompilerParams(vmem_limit_bytes=58 * 1024 * 1024),
+        name="hand_over",
+    )(ent_grad, rel_grad)
     return (ent_grad, rel_grad.reshape(rel_own, out_rows, width))
 
 

time: 85.6 us -> 101 us (1.18)
  the two profiles are of different devices: /device:TPU:4 before, /device:TPU:0 now
where the time goes in v1:
time: 101 us; the launch traced here: 100 us
  Pallas kernels  99.3 us (98%)
    pallas_call x1, Pallas kernels, shards(): pl.pallas_call(functools.partial(kernel, dims), out_shape=(jax.ShapeDtype...  74.4 us
    pallas_call x1, Pallas kernels, shards(): pl.pallas_call(hand_over, out_shape=(jax.ShapeDtypeStruct(ent_grad.shape,...  24.9 us

profile of v1, /device:TPU:0, one launch (start us, length us, event | category | flops | bytes accessed | tf_op | source)
XLA Modules:
  0.0 100.0 jit_solution(263823574765359026)
XLA Ops:
  0.6 74.4 %train_step.1 = (f32[256,256]{1,0:T(8,128)}, f32[512,256]{1,0:T(8,128)}) custom-call(bf16[1024,256]{1,0:T(8,128)(2,1)} %ent.1, bf16[16,256,256]{2,1,0:T(8,128)(2,1)} %ops.1, s32[3,1,1,512]{3,2,1,0:T(1,128)} %left_rows.1, s32[3,1,1,512]{3,2,1,0:T(1,128)} %right_rows.1, s32[3,1,1,1024]{3,2,1,0:T(1,128)} %negatives.1, s32[3,1,1,64]{3,2,1,0:T(1,128)} %counts.1), custom_call_target="tpu_custom_call" | custom-call | tf_op jit(solution)/shard_map/train_step/pallas_call | solution.py:357
  75.0 24.9 %hand_over.1 = (f32[256,256]{1,0:T(8,128)}, f32[512,256]{1,0:T(8,128)}) custom-call(f32[256,256]{1,0:T(8,128)} %get-tuple-element.6.ent_grad, f32[512,256]{1,0:T(8,128)} %get-tuple-element.7.rel_grad), custom_call_target="tpu_custom_call" | custom-call | tf_op jit(solution)/shard_map/hand_over/pallas_call | solution.py:405

commit v2 on v1

--- a/solution.py
+++ b/solution.py
@@ -151,8 +151,9 @@
         meta_copies.append(
             send(meta_send.at[peer[1]], meta.at[offset], meta_ss.at[offset], meta_rs.at[offset], peer)
         )
-    slab_copies = [
-        send(ent, slabs.at[b - 1], slab_ss.at[b - 1], slab_rs.at[b - 1], dom_peer(-b))
+    part = pl.ds(pl.multiple_of(span * own_rows, own_rows), own_rows)
+    slab_parts = [
+        send(ent.at[part], slabs.at[b - 1, part], slab_ss.at[b - 1, 0], slab_rs.at[b - 1, 0], dom_peer(-b))
         for b in range(1, buckets)
     ]
     meta[0] = meta_send[span]
@@ -180,6 +181,19 @@
             onehot[bucket, chunk * block : (chunk + 1) * block, :] = jnp.where(hit, 1.0, 0.0).astype(BF16)
         picked = dot(onehot[bucket], ent[...], ((1,), (0,)))
         lefts[:, bucket * share : (bucket + 1) * share, :] = picked.reshape(rel_own, share, width)
+    slab_copies = []
+    for b in range(1, buckets):
+        slab_parts[b - 1].wait()
+        for offset in range(1, groups):
+            slab_copies.append(
+                send(
+                    slabs.at[b - 1, part],
+                    slabs.at[b - 1, part],
+                    slab_ss.at[b - 1, offset],
+                    slab_rs.at[b - 1, offset],
+                    span_peer(offset),
+                )
+            )
     for rel in range(rel_own):
         queries[rel] = rounded(dot(lefts[rel].astype(BF16), ops[rel], ((1,), (0,))))
 
@@ -281,13 +295,11 @@
             total = total + grad_recv[bucket, offset].astype(F32)
         return total
 
-    score(0, 0)
-    score(1, 0)
+    for chunk in range(chunks):
+        score(chunk, 0)
     for copy in slab_copies:
         copy.wait()
     for chunk in range(chunks):
-        if chunk > 1:
-            score(chunk, 0)
         for bucket in range(1, buckets):
             score(chunk, bucket)
         send_pair(chunk)
@@ -302,14 +314,14 @@
 
     home_copies = []
     for bucket in range(1, buckets):
-        home_send[bucket] = gathered(bucket, grad_copies[bucket])
+        home_send[bucket] = gathered(bucket, grad_copies[bucket]).astype(BF16)
         home_copies.append(
             send(home_send.at[bucket], home_recv.at[bucket], home_ss.at[bucket], home_rs.at[bucket], dom_peer(bucket))
         )
     total = gathered(0, grad_copies[0])
     for bucket in range(1, buckets):
         home_copies[bucket - 1].wait()
-        total = total + home_recv[bucket]
+        total = total + home_recv[bucket].astype(F32)
     ent_out[...] = total
 
     for chunk in range(chunks):
@@ -322,15 +334,9 @@
         rel_out[rows, :] = total
 
 
-def hand_over(ent_grad, rel_grad, ent_out, rel_out, sems):
-    copies = [
-        pltpu.make_async_copy(ent_grad, ent_out, sems.at[0]),
-        pltpu.make_async_copy(rel_grad, rel_out, sems.at[1]),
-    ]
-    for copy in copies:
-        copy.start()
-    for copy in copies:
-        copy.wait()
+def hand_over(ent_grad, rel_grad, ent_out, rel_out):
+    ent_out[...] = ent_grad[...]
+    rel_out[...] = rel_grad[...]
 
 
 def shards(entities, operators, left_rows, right_rows, negatives, counts):
@@ -376,8 +382,8 @@
             pltpu.VMEM((buckets, part_rows, width), F32),
             pltpu.VMEM((buckets, groups, own_rows, width), BF16),
             pltpu.VMEM((buckets, groups, own_rows, width), BF16),
-            pltpu.VMEM((buckets, own_rows, width), F32),
-            pltpu.VMEM((buckets, own_rows, width), F32),
+            pltpu.VMEM((buckets, own_rows, width), BF16),
+            pltpu.VMEM((buckets, own_rows, width), BF16),
             pltpu.VMEM((2, levels, rel_own * out_rows, width), F32),
             pltpu.VMEM((chunks, levels, chunk_rows, width), BF16),
             pltpu.VMEM((chunks, levels, chunk_rows, width), BF16),
@@ -385,8 +391,8 @@
             pltpu.VMEM((chunks, levels, chunk_rows, width), BF16),
             dma((groups,)),
             dma((groups,)),
-            dma((buckets - 1,)),
-            dma((buckets - 1,)),
+            dma((buckets - 1, groups)),
+            dma((buckets - 1, groups)),
             dma((buckets, groups)),
             dma((buckets, groups)),
             dma((buckets,)),
@@ -401,17 +407,14 @@
         ),
         name="train_step",
     )(entities, operators, left_rows, right_rows, negatives, counts)
-    anywhere = pl.BlockSpec(memory_space=pl.ANY)
     ent_grad, rel_grad = pl.pallas_call(
         hand_over,
         out_shape=(
             jax.ShapeDtypeStruct(ent_grad.shape, F32),
             jax.ShapeDtypeStruct(rel_grad.shape, F32),
         ),
-        in_specs=[anywhere] * 2,
-        out_specs=(anywhere, anywhere),
-        scratch_shapes=[dma((2,))],
-        compiler_params=pltpu.CompilerParams(vmem_limit_bytes=58 * 1024 * 1024),
+        in_specs=[vmem] * 2,
+        out_specs=(vmem, vmem),
         name="hand_over",
     )(ent_grad, rel_grad)
     return (ent_grad, rel_grad.reshape(rel_own, out_rows, width))

time: 101 us -> 68.5 us (0.68)
  Pallas kernels: 99.3 us -> 66.8 us
    pallas_call x1, Pallas kernels: 24.9 us -> 2.02 us  [shards(): pl.pallas_call(hand_over, out_shape=(jax.ShapeDtypeStruct(ent_grad.shape,...]
    pallas_call x1, Pallas kernels: 74.4 us -> 64.7 us  [shards(): pl.pallas_call(functools.partial(kernel, dims), out_shape=(jax.ShapeDtype...]
where the time goes in v2:
time: 68.5 us; the launch traced here: 67.4 us
  Pallas kernels  66.8 us (98%)
    pallas_call x1, Pallas kernels, shards(): pl.pallas_call(functools.partial(kernel, dims), out_shape=(jax.ShapeDtype...  64.7 us
    pallas_call x1, Pallas kernels, shards(): pl.pallas_call(hand_over, out_shape=(jax.ShapeDtypeStruct(ent_grad.shape,...  2.02 us

profile of v2, /device:TPU:0, one launch (start us, length us, event | category | flops | bytes accessed | tf_op | source)
XLA Modules:
  0.0 67.4 jit_solution(4984893103270877452)
XLA Ops:
  0.6 64.7 %train_step.1 = (f32[256,256]{1,0:T(8,128)}, f32[512,256]{1,0:T(8,128)}) custom-call(bf16[1024,256]{1,0:T(8,128)(2,1)} %ent.1, bf16[16,256,256]{2,1,0:T(8,128)(2,1)} %ops.1, s32[3,1,1,512]{3,2,1,0:T(1,128)} %left_rows.1, s32[3,1,1,512]{3,2,1,0:T(1,128)} %right_rows.1, s32[3,1,1,1024]{3,2,1,0:T(1,128)} %negatives.1, s32[3,1,1,64]{3,2,1,0:T(1,128)} %counts.1), custom_call_target="tpu_custom_call" | custom-call | tf_op jit(solution)/shard_map/train_step/pallas_call | solution.py:363
  65.4 2.0 %hand_over.1 = (f32[256,256]{1,0:T(8,128)}, f32[512,256]{1,0:T(8,128)}) custom-call(f32[256,256]{1,0:T(8,128)} %get-tuple-element.6.ent_grad, f32[512,256]{1,0:T(8,128)} %get-tuple-element.7.rel_grad), custom_call_target="tpu_custom_call" | custom-call | tf_op jit(solution)/shard_map/hand_over/pallas_call | solution.py:410

commit v3 on v2

--- a/solution.py
+++ b/solution.py
@@ -43,6 +43,7 @@
     query_grads,
     acc,
     own_grad,
+    pair_recv,
     grad_send,
     grad_recv,
     home_send,
@@ -56,6 +57,8 @@
     meta_rs,
     slab_ss,
     slab_rs,
+    pair_ss,
+    pair_rs,
     grad_ss,
     grad_rs,
     home_ss,
@@ -65,7 +68,7 @@
     z_ss,
     z_rs,
 ):
-    buckets, doms, groups, rel_own, cap, chunks = dims
+    buckets, doms, groups, rel_own, cap, chunks, pieces = dims
     part_rows, width = ent.shape
     slot_count = left_rows.shape[-1]
     neg_count = negatives.shape[-1]
@@ -75,7 +78,9 @@
     own_rows = part_rows // groups
     out_rows = width // doms
     chunk_rels = rel_own // chunks
-    chunk_rows = chunk_rels * out_rows
+    piece_rels = chunk_rels // pieces
+    piece_rows = piece_rels * out_rows
+    half = groups // 2
     share = groups * cap
     block = chunk_rels * share
     mult_rows = part_rows // LANES
@@ -84,6 +89,8 @@
     span = lax.axis_index("span")
     y = lax.rem(dom, 2)
     z = lax.div(dom, 2)
+    core = lax.rem(span, 2)
+    chip = lax.div(span, 2)
 
     def span_peer(offset):
         return (dom, lax.rem(span + offset, groups))
@@ -184,8 +191,9 @@
     slab_copies = []
     for b in range(1, buckets):
         slab_parts[b - 1].wait()
+        slab_copies.append([])
         for offset in range(1, groups):
-            slab_copies.append(
+            slab_copies[b - 1].append(
                 send(
                     slabs.at[b - 1, part],
                     slabs.at[b - 1, part],
@@ -225,35 +233,35 @@
 
     y_copies = []
 
-    def send_pair(chunk):
-        for rel in range(chunk * chunk_rels, (chunk + 1) * chunk_rels):
+    def send_pair(piece):
+        for rel in range(piece * piece_rels, (piece + 1) * piece_rels):
             outer = dot(lefts[rel].astype(BF16), query_grads[rel].astype(BF16), ((0,), (0,)))
             for level in range(levels):
                 for side in range(2):
                     first = (level * 2 + side) * out_rows
                     rel_acc[side, level, rel * out_rows : (rel + 1) * out_rows, :] = outer[first : first + out_rows]
-        rows = slice(chunk * chunk_rows, (chunk + 1) * chunk_rows)
-        y_send[chunk] = rel_acc[1 - y, :, rows, :].astype(BF16)
+        rows = slice(piece * piece_rows, (piece + 1) * piece_rows)
+        y_send[piece] = rel_acc[1 - y, :, rows, :].astype(BF16)
         y_copies.append(
-            send(y_send.at[chunk], y_recv.at[chunk], y_ss.at[chunk], y_rs.at[chunk], (dom + 1 - 2 * y, span))
+            send(y_send.at[piece], y_recv.at[piece], y_ss.at[piece], y_rs.at[piece], (dom + 1 - 2 * y, span))
         )
 
     z_copies = []
 
-    def send_level(chunk):
-        y_copies[chunk].wait()
-        rows = slice(chunk * chunk_rows, (chunk + 1) * chunk_rows)
-        total = rel_acc[y, :, rows, :] + y_recv[chunk].astype(F32)
+    def send_level(piece):
+        y_copies[piece].wait()
+        rows = slice(piece * piece_rows, (piece + 1) * piece_rows)
+        total = rel_acc[y, :, rows, :] + y_recv[piece].astype(F32)
         rel_acc[y, :, rows, :] = total
-        z_send[chunk] = total.astype(BF16)
+        z_send[piece] = total.astype(BF16)
         for offset in range(1, levels):
             level = lax.rem(z + offset, levels)
             z_copies.append(
                 send(
-                    z_send.at[chunk, level],
-                    z_recv.at[chunk, offset],
-                    z_ss.at[chunk, offset],
-                    z_rs.at[chunk, offset],
+                    z_send.at[piece, level],
+                    z_recv.at[piece, offset],
+                    z_ss.at[piece, offset],
+                    z_rs.at[piece, offset],
                     (level * 2 + y, span),
                 )
             )
@@ -268,69 +276,96 @@
         rows = jnp.concatenate(rows, axis=0).astype(BF16)
         acc[0] += dot(rows, jnp.concatenate(marks, axis=0), ((0,), (0,)))
 
-    def send_grads(bucket):
+    pair_copies = {}
+    chip_copies = {}
+    home_copies = {}
+
+    def send_core(bucket):
         total = jnp.transpose(acc[bucket])
-        own_grad[bucket] = total
         for holder in range(groups):
-            grad_send[bucket, holder] = total[holder * own_rows : (holder + 1) * own_rows].astype(BF16)
-        copies = []
-        for offset in range(1, groups):
-            peer = span_peer(offset)
-            copies.append(
+            own_grad[bucket, holder % 2, holder // 2] = total[holder * own_rows : (holder + 1) * own_rows]
+        pair_copies[bucket] = send(
+            own_grad.at[bucket, 1 - core],
+            pair_recv.at[bucket],
+            pair_ss.at[bucket],
+            pair_rs.at[bucket],
+            (dom, span + 1 - 2 * core),
+        )
+
+    def send_chip(bucket):
+        pair_copies[bucket].wait()
+        total = own_grad[bucket, core] + pair_recv[bucket]
+        own_grad[bucket, core] = total
+        grad_send[bucket] = total.astype(BF16)
+        chip_copies[bucket] = []
+        for offset in range(1, half):
+            to_chip = lax.rem(chip + offset, half)
+            chip_copies[bucket].append(
                 send(
-                    grad_send.at[bucket, peer[1]],
+                    grad_send.at[bucket, to_chip],
                     grad_recv.at[bucket, offset],
                     grad_ss.at[bucket, offset],
                     grad_rs.at[bucket, offset],
-                    peer,
+                    (dom, to_chip * 2 + core),
                 )
             )
-        return copies
-
-    def gathered(bucket, copies):
-        for copy in copies:
+
+    def gathered(bucket):
+        for copy in chip_copies[bucket]:
             copy.wait()
-        total = own_grad[bucket, pl.ds(pl.multiple_of(span * own_rows, own_rows), own_rows), :]
-        for offset in range(1, groups):
+        total = own_grad[bucket, core, chip]
+        for offset in range(1, half):
             total = total + grad_recv[bucket, offset].astype(F32)
         return total
 
+    def send_home(bucket):
+        home_send[bucket] = gathered(bucket).astype(BF16)
+        home_copies[bucket] = send(
+            home_send.at[bucket], home_recv.at[bucket], home_ss.at[bucket], home_rs.at[bucket], dom_peer(bucket)
+        )
+
+    last = chunks - 1
     for chunk in range(chunks):
         score(chunk, 0)
-    for copy in slab_copies:
-        copy.wait()
     for chunk in range(chunks):
         for bucket in range(1, buckets):
+            if chunk == 0:
+                for copy in slab_copies[bucket - 1]:
+                    copy.wait()
             score(chunk, bucket)
-        send_pair(chunk)
+            if chunk == last and bucket < buckets - 1:
+                send_core(bucket)
+        for piece in range(chunk * pieces, (chunk + 1) * pieces):
+            send_pair(piece)
+        if chunk == last:
+            send_core(buckets - 1)
         if chunk > 0:
-            send_level(chunk - 1)
-        if chunk < chunks - 1:
+            for piece in range((chunk - 1) * pieces, chunk * pieces):
+                send_level(piece)
+        if chunk < last:
             left_part(chunk)
-    grad_copies = [None] + [send_grads(bucket) for bucket in range(1, buckets)]
-    left_part(chunks - 1)
-    grad_copies[0] = send_grads(0)
-    send_level(chunks - 1)
-
-    home_copies = []
     for bucket in range(1, buckets):
-        home_send[bucket] = gathered(bucket, grad_copies[bucket]).astype(BF16)
-        home_copies.append(
-            send(home_send.at[bucket], home_recv.at[bucket], home_ss.at[bucket], home_rs.at[bucket], dom_peer(bucket))
-        )
-    total = gathered(0, grad_copies[0])
+        send_chip(bucket)
+    left_part(last)
+    send_core(0)
     for bucket in range(1, buckets):
-        home_copies[bucket - 1].wait()
+        send_home(bucket)
+    for piece in range(last * pieces, chunks * pieces):
+        send_level(piece)
+    send_chip(0)
+    total = gathered(0)
+    for bucket in range(1, buckets):
+        home_copies[bucket].wait()
         total = total + home_recv[bucket].astype(F32)
     ent_out[...] = total
 
-    for chunk in range(chunks):
-        for copy in z_copies[chunk * (levels - 1) : (chunk + 1) * (levels - 1)]:
+    for piece in range(chunks * pieces):
+        for copy in z_copies[piece * (levels - 1) : (piece + 1) * (levels - 1)]:
             copy.wait()
-        rows = slice(chunk * chunk_rows, (chunk + 1) * chunk_rows)
+        rows = slice(piece * piece_rows, (piece + 1) * piece_rows)
         total = rel_acc[y, z, rows, :]
         for offset in range(1, levels):
-            total = total + z_recv[chunk, offset].astype(F32)
+            total = total + z_recv[piece, offset].astype(F32)
         rel_out[rows, :] = total
 
 
@@ -353,11 +388,13 @@
     out_rows = width // doms
     levels = doms // 2
     chunks = 4 if (rel_own // 4) * out_rows % 16 == 0 else 2
-    chunk_rows = rel_own // chunks * out_rows
+    pieces = 2 if (rel_own // chunks // 2) * out_rows % 16 == 0 else 1
+    piece_rows = rel_own // chunks // pieces * out_rows
+    half = groups // 2
     mult_rows = part_rows // LANES
     meta_rows = MULT_AT + -(-buckets * mult_rows // 8) * 8
     edges = buckets * groups * cap
-    dims = (buckets, doms, groups, rel_own, cap, chunks)
+    dims = (buckets, doms, groups, rel_own, cap, chunks, pieces)
     dma = pltpu.SemaphoreType.DMA
     vmem = pl.BlockSpec(memory_space=pltpu.VMEM)
     ent_grad, rel_grad = pl.pallas_call(
@@ -379,28 +416,31 @@
             pltpu.VMEM((rel_own, edges, width), F32),
             pltpu.VMEM((rel_own, edges, width), F32),
             pltpu.VMEM((buckets, width, part_rows), F32),
-            pltpu.VMEM((buckets, part_rows, width), F32),
-            pltpu.VMEM((buckets, groups, own_rows, width), BF16),
-            pltpu.VMEM((buckets, groups, own_rows, width), BF16),
+            pltpu.VMEM((buckets, 2, half, own_rows, width), F32),
+            pltpu.VMEM((buckets, half, own_rows, width), F32),
+            pltpu.VMEM((buckets, half, own_rows, width), BF16),
+            pltpu.VMEM((buckets, half, own_rows, width), BF16),
             pltpu.VMEM((buckets, own_rows, width), BF16),
             pltpu.VMEM((buckets, own_rows, width), BF16),
             pltpu.VMEM((2, levels, rel_own * out_rows, width), F32),
-            pltpu.VMEM((chunks, levels, chunk_rows, width), BF16),
-            pltpu.VMEM((chunks, levels, chunk_rows, width), BF16),
-            pltpu.VMEM((chunks, levels, chunk_rows, width), BF16),
-            pltpu.VMEM((chunks, levels, chunk_rows, width), BF16),
+            pltpu.VMEM((chunks * pieces, levels, piece_rows, width), BF16),
+            pltpu.VMEM((chunks * pieces, levels, piece_rows, width), BF16),
+            pltpu.VMEM((chunks * pieces, levels, piece_rows, width), BF16),
+            pltpu.VMEM((chunks * pieces, levels, piece_rows, width), BF16),
             dma((groups,)),
             dma((groups,)),
             dma((buckets - 1, groups)),
             dma((buckets - 1, groups)),
-            dma((buckets, groups)),
-            dma((buckets, groups)),
             dma((buckets,)),
             dma((buckets,)),
-            dma((chunks,)),
-            dma((chunks,)),
-            dma((chunks, levels)),
-            dma((chunks, levels)),
+            dma((buckets, half)),
+            dma((buckets, half)),
+            dma((buckets,)),
+            dma((buckets,)),
+            dma((chunks * pieces,)),
+            dma((chunks * pieces,)),
+            dma((chunks * pieces, levels)),
+            dma((chunks * pieces, levels)),
         ],
         compiler_params=pltpu.CompilerParams(
             collective_id=0, has_side_effects=True, vmem_limit_bytes=58 * 1024 * 1024

time: 68.5 us -> 66.5 us (0.971); the launches traced: 67.4 us -> 66.3 us
  Pallas kernels: 66.8 us -> 65.7 us
    pallas_call x1, Pallas kernels: 64.7 us -> 63.7 us  [shards(): pl.pallas_call(functools.partial(kernel, dims), out_shape=(jax.ShapeDtype...]
where the time goes in v3:
time: 66.5 us; the launch traced here: 66.3 us
  Pallas kernels  65.7 us (99%)
    pallas_call x1, Pallas kernels, shards(): pl.pallas_call(functools.partial(kernel, dims), out_shape=(jax.ShapeDtype...  63.7 us
    pallas_call x1, Pallas kernels, shards(): pl.pallas_call(hand_over, out_shape=(jax.ShapeDtypeStruct(ent_grad.shape,...  2.02 us

profile of v3, /device:TPU:0, one launch (start us, length us, event | category | flops | bytes accessed | tf_op | source)
XLA Modules:
  0.0 66.3 jit_solution(5038293112622641765)
XLA Ops:
  0.6 63.7 %train_step.1 = (f32[256,256]{1,0:T(8,128)}, f32[512,256]{1,0:T(8,128)}) custom-call(bf16[1024,256]{1,0:T(8,128)(2,1)} %ent.1, bf16[16,256,256]{2,1,0:T(8,128)(2,1)} %ops.1, s32[3,1,1,512]{3,2,1,0:T(1,128)} %left_rows.1, s32[3,1,1,512]{3,2,1,0:T(1,128)} %right_rows.1, s32[3,1,1,1024]{3,2,1,0:T(1,128)} %negatives.1, s32[3,1,1,64]{3,2,1,0:T(1,128)} %counts.1), custom_call_target="tpu_custom_call" | custom-call | tf_op jit(solution)/shard_map/train_step/pallas_call | solution.py:400
  64.3 2.0 %hand_over.1 = (f32[256,256]{1,0:T(8,128)}, f32[512,256]{1,0:T(8,128)}) custom-call(f32[256,256]{1,0:T(8,128)} %get-tuple-element.6.ent_grad, f32[512,256]{1,0:T(8,128)} %get-tuple-element.7.rel_grad), custom_call_target="tpu_custom_call" | custom-call | tf_op jit(solution)/shard_map/hand_over/pallas_call | solution.py:450

commit v4 on v3

--- a/solution.py
+++ b/solution.py
@@ -178,8 +178,8 @@
             )
             times[bucket, group * cap : (group + 1) * cap, :] = jnp.broadcast_to(mult, (cap, part_rows))
 
-    def column(chunk, which):
-        held = cols[chunk * chunk_rels : (chunk + 1) * chunk_rels].reshape(block, MULT_AT)
+    def column(chunk, which, wide=1):
+        held = cols[chunk * chunk_rels : (chunk + wide) * chunk_rels].reshape(wide * block, MULT_AT)
         return held[:, which : which + 1]
 
     for bucket in range(buckets):
@@ -189,7 +189,8 @@
         picked = dot(onehot[bucket], ent[...], ((1,), (0,)))
         lefts[:, bucket * share : (bucket + 1) * share, :] = picked.reshape(rel_own, share, width)
     slab_copies = []
-    for b in range(1, buckets):
+
+    def pass_on(b):
         slab_parts[b - 1].wait()
         slab_copies.append([])
         for offset in range(1, groups):
@@ -202,28 +203,32 @@
                     span_peer(offset),
                 )
             )
+
     for rel in range(rel_own):
         queries[rel] = rounded(dot(lefts[rel].astype(BF16), ops[rel], ((1,), (0,))))
 
-    def score(chunk, bucket):
+    def score(chunk, bucket, wide=1):
+        edges = wide * block
+        many = wide * chunk_rels
+        lane_row = lax.broadcasted_iota(jnp.int32, (edges, part_rows), 1).astype(F32)
         right = ent if bucket == 0 else slabs.at[bucket - 1]
-        rels = slice(chunk * chunk_rels, (chunk + 1) * chunk_rels)
+        rels = slice(chunk * chunk_rels, (chunk + wide) * chunk_rels)
         at = slice(bucket * share, (bucket + 1) * share)
-        query = queries[rels, at, :].reshape(block, width).astype(BF16)
-        live_col = column(chunk, 2 * buckets + bucket)
+        query = queries[rels, at, :].reshape(edges, width).astype(BF16)
+        live_col = column(chunk, 2 * buckets + bucket, wide)
         scores = dot(query, right[...], ((1,), (1,)))
-        hit = lane_row == column(chunk, buckets + bucket)
+        hit = lane_row == column(chunk, buckets + bucket, wide)
         positive = jnp.sum(jnp.where(hit, scores, 0.0), axis=1, keepdims=True)
         pos_grad = -live_col * jax.nn.sigmoid(-positive)
         neg_grad = rounded((jnp.tanh(scores * 0.5) + 1.0) * (live_col * (0.5 * neg_scale)))
-        counted = neg_grad.reshape(chunk_rels, share, part_rows) * times[bucket][None]
-        weight = counted.reshape(block, part_rows) + jnp.where(hit, pos_grad, 0.0)
+        counted = neg_grad.reshape(many, share, part_rows) * times[bucket][None]
+        weight = counted.reshape(edges, part_rows) + jnp.where(hit, pos_grad, 0.0)
         high = weight.astype(BF16)
         low = (weight - high.astype(F32)).astype(BF16)
         both = jnp.concatenate([high, low], axis=0)
         parts = dot(both, right[...], ((1,), (0,)))
-        query_grad = rounded(parts[0:block] + parts[block:])
-        query_grads[rels, at, :] = query_grad.reshape(chunk_rels, share, width)
+        query_grad = rounded(parts[0:edges] + parts[edges:])
+        query_grads[rels, at, :] = query_grad.reshape(many, share, width)
         twice = jnp.concatenate([query, query], axis=0)
         slab_grad = dot(twice, both, ((0,), (0,)))
         if chunk == 0:
@@ -325,16 +330,23 @@
         )
 
     last = chunks - 1
-    for chunk in range(chunks):
-        score(chunk, 0)
+    pass_on(1)
+    for chunk in range(0, chunks, 2):
+        score(chunk, 0, 2)
+        if chunk == 0:
+            for bucket in range(2, buckets):
+                pass_on(bucket)
     for chunk in range(chunks):
         for bucket in range(1, buckets):
             if chunk == 0:
                 for copy in slab_copies[bucket - 1]:
                     copy.wait()
-            score(chunk, bucket)
-            if chunk == last and bucket < buckets - 1:
-                send_core(bucket)
+            if bucket == buckets - 1:
+                score(chunk, bucket)
+            elif chunk % 2 == 0:
+                score(chunk, bucket, 2)
+                if chunk == last - 1:
+                    send_core(bucket)
         for piece in range(chunk * pieces, (chunk + 1) * pieces):
             send_pair(piece)
         if chunk == last:

time: 66.5 us -> 66.5 us (level)
  no operation moved by 1% of the time
where the time goes in v4:
time: 66.5 us; the launch traced here: 66.3 us
  Pallas kernels  65.7 us (99%)
    pallas_call x1, Pallas kernels, shards(): pl.pallas_call(functools.partial(kernel, dims), out_shape=(jax.ShapeDtype...  63.6 us
    pallas_call x1, Pallas kernels, shards(): pl.pallas_call(hand_over, out_shape=(jax.ShapeDtypeStruct(ent_grad.shape,...  2.02 us

profile of v4, /device:TPU:0, one launch (start us, length us, event | category | flops | bytes accessed | tf_op | source)
XLA Modules:
  0.0 66.3 jit_solution(5844973568734294080)
XLA Ops:
  0.6 63.6 %train_step.1 = (f32[256,256]{1,0:T(8,128)}, f32[512,256]{1,0:T(8,128)}) custom-call(bf16[1024,256]{1,0:T(8,128)(2,1)} %ent.1, bf16[16,256,256]{2,1,0:T(8,128)(2,1)} %ops.1, s32[3,1,1,512]{3,2,1,0:T(1,128)} %left_rows.1, s32[3,1,1,512]{3,2,1,0:T(1,128)} %right_rows.1, s32[3,1,1,1024]{3,2,1,0:T(1,128)} %negatives.1, s32[3,1,1,64]{3,2,1,0:T(1,128)} %counts.1), custom_call_target="tpu_custom_call" | custom-call | tf_op jit(solution)/shard_map/train_step/pallas_call | solution.py:412
  64.3 2.0 %hand_over.1 = (f32[256,256]{1,0:T(8,128)}, f32[512,256]{1,0:T(8,128)}) custom-call(f32[256,256]{1,0:T(8,128)} %get-tuple-element.6.ent_grad, f32[512,256]{1,0:T(8,128)} %get-tuple-element.7.rel_grad), custom_call_target="tpu_custom_call" | custom-call | tf_op jit(solution)/shard_map/hand_over/pallas_call | solution.py:462
